TPU v7x, 32 devices: a whole 2x2x4 slice. The times are simulated.
32 devices in a mesh: wall: 4 (over x, core), surf: 8 (over z, y).
Axes of the slice: x: 2, y: 2, z: 4, core: 2. Of those that a mesh axis runs over, the one named last changes fastest.
Arguments:
- primal: bfloat16 [6, 128, 8192], P(None, 'wall', 'surf'), may hold values from -6 to 6
- adjoint: bfloat16 [6, 128, 8192], P(None, 'wall', 'surf'), may hold values from -6 to 6
- coords: float32 [3, 128, 8192], P(None, 'wall', 'surf'), may hold values from -6 to 6
- foot_index: int32 [2, 128, 8192], P(None, 'wall', 'surf'), may hold values from 0 to 15
- foot_weight: float32 [2, 128, 8192], P(None, 'wall', 'surf'), may hold values from 0.002 to 0.02
- blanking: int32 [128, 8192], P('wall', 'surf'), may hold values 0 or 1
- owner_map: int32 [8192], replicated, may hold values from 0 to 8191, as said below
Outputs:
- surface_sens: float32 [3, 8192], P(None, 'surf')
Inputs may be any that keep to these rules, and one draw needn't show every extreme that they name: `owner_map`: each control point is named by exactly one output slot; slot c * 1024 + b * 128 + i, for i below 128, names a control point of the aligned block b of 1024 control points. `foot_index`: offsets of control points from a grid point's column, plus 8.
All inputs are finite; a program needn't handle non-finite values. No bound on the sum of `blanking` on one device may be relied on, other than what follows from the above.
Results may differ from a plain program's by a relative error of at most 0.0003.
Values may be sent and summed in bfloat16 or wider, within the bound.
A program may use at most 128 MiB of HBM per device.

v0:
```python
import jax
import jax.numpy as jnp
from jax import lax
from jax.sharding import PartitionSpec as P


def padded(shard, sides, width):
    for axis, dim in sides:
        devices, length = (lax.axis_size(axis), shard.shape[dim])
        up = [(i, (i + 1) % devices) for i in range(devices - 1)]
        down = [(j, i) for i, j in up]
        last = lax.slice_in_dim(shard, length - width, length, axis=dim)
        leading = lax.slice_in_dim(shard, 0, width, axis=dim)
        before = lax.ppermute(last, axis, up)
        after = lax.ppermute(leading, axis, down)
        shard = jnp.concatenate([before, shard, after], axis=dim)
    return shard


def face_term(q_low, q_high, a_low, a_high, x_low, x_high):
    average = 0.5 * (q_low + q_high)
    jump = q_high - q_low
    adjoint_jump = a_low - a_high
    face_normal = x_high - x_low
    along_sum = jnp.sum(adjoint_jump * average, axis=0)
    across_sum = jnp.sum(adjoint_jump * jump, axis=0)
    return along_sum * average[1:4] + average[4] * adjoint_jump[1:4] - across_sum * face_normal


def body(primal, adjoint, coords, foot_index, foot_weight, blanking, owner_map):
    layers = primal.shape[1]
    columns = primal.shape[2]
    fields = jnp.concatenate([primal, adjoint], axis=0)
    padded_fields = padded(fields, (("wall", 1), ("surf", 2)), 1).astype(jnp.float32)
    padded_coords = padded(coords, (("wall", 1), ("surf", 2)), 1)
    q_cols = padded_fields[:6, :, 1 : columns + 1]
    a_cols = padded_fields[6:, :, 1 : columns + 1]
    x_cols = padded_coords[:, :, 1 : columns + 1]
    wall_h = face_term(
        q_cols[:, :-1], q_cols[:, 1:], a_cols[:, :-1], a_cols[:, 1:], x_cols[:, :-1], x_cols[:, 1:]
    )
    sensitivity = wall_h[:, :-1] - wall_h[:, 1:]
    q_rows = padded_fields[:6, 1 : layers + 1]
    a_rows = padded_fields[6:, 1 : layers + 1]
    x_rows = padded_coords[:, 1 : layers + 1]
    surf_h = face_term(
        q_rows[:, :, :-1],
        q_rows[:, :, 1:],
        a_rows[:, :, :-1],
        a_rows[:, :, 1:],
        x_rows[:, :, :-1],
        x_rows[:, :, 1:],
    )
    sensitivity = sensitivity + surf_h[:, :, :-1] - surf_h[:, :, 1:]
    weighted = blanking.astype(jnp.float32)[None] * foot_weight
    window = jnp.zeros((3, columns + 16), jnp.float32)
    for offset in range(16):
        picked = jnp.sum(jnp.where(foot_index == offset, weighted, 0.0), axis=0)
        contrib = jnp.sum(picked[None] * sensitivity, axis=1)
        window = window.at[:, offset : offset + columns].add(contrib)
    total_points = owner_map.shape[0]
    my_block = lax.axis_index("surf")
    start = my_block * columns
    spread = lax.dynamic_update_slice_in_dim(
        jnp.zeros((3, total_points + 16), jnp.float32), window, start, 1
    )
    point_buffer = spread[:, 8 : total_points + 8]
    point_buffer = point_buffer.at[:, :8].add(spread[:, total_points + 8 :])
    point_buffer = point_buffer.at[:, total_points - 8 :].add(spread[:, :8])
    summed = lax.psum(point_buffer, ("wall", "surf"))
    my_slots = lax.dynamic_slice_in_dim(owner_map, start, columns, 0)
    return summed[:, my_slots]


def solution(mesh):
    placed = (
        P(None, "wall", "surf"),
        P(None, "wall", "surf"),
        P(None, "wall", "surf"),
        P(None, "wall", "surf"),
        P(None, "wall", "surf"),
        P("wall", "surf"),
        P(),
    )
    return jax.shard_map(
        body, mesh=mesh, in_specs=placed, out_specs=P(None, "surf"), check_vma=False
    )
```

profile of v0, /device:TPU:0, one launch (start us, length us, event | category | flops | bytes accessed | tf_op | source)
XLA Modules:
  0.0 283.1 jit_solution(12398395438387048853)
XLA Ops:
  8.7 2.4 collective-permute-start
  14.7 5.8 %collective-permute-start.5 = (f32[3,1,1024]{2,1,0:T(1,128)S(1)}, f32[3,1,1024]{2,1,0:T(1,128)S(1)}, u32[]{:S(2)}, u32[]{:S(2)}) collective-permute-start(f32[3,1,1024]{2,1,0:T(1,128)S(1)} %get-tuple-element.267), channel_id=1, source_target_pairs={{0,8},{8,16},{16,24},{1,9},{9,17},{17,25},{2,10},{10,18},{18,26},{... | collective-permute-start | bytes 36872 | tf_op jit(solution)/shard_map/ppermute | solution.py:14
  21.4 2.7 select_reduce_fusion
  36.2 3.4 %collective-permute-start.2 = (bf16[12,34,1]{2,1,0:T(8,128)(2,1)S(1)}, bf16[12,34,1]{2,1,0:T(8,128)(2,1)S(1)}, u32[]{:S(2)}, u32[]{:S(2)}) collective-permute-start(bf16[12,34,1]{2,1,0:T(8,128)(2,1)S(1)} %get-tuple-element.262), channel_id=1, source_target_pairs={{0,1},{1,2},{2,3},{3,4},{4,5},{5,6},{6,7},{8,9},{9,10},{10,11},{11... | collective-permute-start | bytes 2456 | tf_op jit(solution)/shard_map/ppermute | solution.py:14
  43.0 5.8 %collective-permute-start.7 = (f32[3,34,1]{2,1,0:T(8,128)}, f32[3,34,1]{2,1,0:T(8,128)}, u32[]{:S(2)}, u32[]{:S(2)}) collective-permute-start(f32[3,34,1]{2,1,0:T(8,128)} %get-tuple-element.266), channel_id=1, source_target_pairs={{0,1},{1,2},{2,3},{3,4},{4,5},{5,6},{6,7},{8,9},{9,10},{10,11},{11... | collective-permute-start | bytes 1232 | tf_op jit(solution)/shard_map/ppermute | solution.py:14
  49.4 2.3 concatenate.63
  72.0 2.0 scatter-add.61
  75.7 2.0 scatter-add.64
  79.5 2.0 scatter-add.65
  83.4 2.0 scatter-add.66
  87.2 2.0 scatter-add.69
  90.9 2.0 scatter-add.70
  94.7 2.0 scatter-add.71
  96.7 1.9 fusion
  100.3 2.0 scatter-add.75
  104.2 2.0 scatter-add.76
  108.0 2.0 scatter-add.79
  110.6 2.0 scatter-add.80
  113.4 2.0 scatter-add.81
  116.1 2.0 scatter-add.84
  118.8 2.0 scatter-add.85
  121.2 2.2 slice.540
  126.7 143.7 %all-reduce.3.cloned.1.call-done = f32[3,8192]{0,1:T(8,128)} async-done(((f32[3,8192]{0,1:T(8,128)}), f32[3,8192]{0,1:T(8,128)}) %all-reduce.3.cloned.1.call-update) | async-done | bytes 98320 | tf_op jit(solution)/shard_map/psum | solution.py:70
  270.4 5.0 %gather_fusion = f32[1024,3]{1,0:T(8,128)S(1)} fusion(f32[3,8192]{0,1:T(8,128)} %all-reduce.3.cloned.1.call-done, s32[1024]{0:T(1024)S(1)} %fusion.9), kind=kCustom, calls=%fused_computation | custom fusion | bytes 28672 | tf_op jit(solution)/shard_map/gather | solution.py:72
  (106 shorter events, 65.3 us)
Async XLA Ops:
  6.5 34.4 %copy-start = (f32[3,32,1024]{2,1,0:T(8,128)S(1)}, f32[3,32,1024]{2,1,0:T(8,128)}, u32[]{:S(2)}) copy-start(f32[3,32,1024]{2,1,0:T(8,128)} %param.45) | copy-start | bytes 1179652
  6.5 263.9 %all-reduce.3.cloned.1.call-start = ((), (), s32[]{:S(2)}) async-start(), calls=%async_computation | async-start | bytes 8388608 | tf_op jit(solution)/shard_map/psum | solution.py:70
  8.7 26.1 %collective-permute-start = (bf16[12,1,1024]{2,1,0:T(2,128)(2,1)S(1)}, bf16[12,1,1024]{2,1,0:T(2,128)(2,1)S(1)}, u32[]{:S(2)}, u32[]{:S(2)}) collective-permute-start(bf16[12,1,1024]{2,1,0:T(2,128)(2,1)S(1)} %get-tuple-element.263), channel_id=1, source_target_pairs={{0,8},{8,16},{16,24},{1,9},{9,17},{17,25},{2,10},{10,18},{18,26},{... | collective-permute-start | bytes 73736 | tf_op jit(solution)/shard_map/ppermute | solution.py:14
  11.1 23.8 %collective-permute-start.1 = (bf16[12,1,1024]{2,1,0:T(2,128)(2,1)S(1)}, bf16[12,1,1024]{2,1,0:T(2,128)(2,1)}, u32[]{:S(2)}, u32[]{:S(2)}) collective-permute-start(bf16[12,1,1024]{2,1,0:T(2,128)(2,1)S(1)} %get-tuple-element.264), channel_id=1, source_target_pairs={{8,0},{16,8},{24,16},{9,1},{17,9},{25,17},{10,2},{18,10},{26,18},{... | collective-permute-start | bytes 73736 | tf_op jit(solution)/shard_map/ppermute | solution.py:15
  13.4 27.6 %collective-permute-start.4 = (f32[3,1,1024]{2,1,0:T(1,128)S(1)}, f32[3,1,1024]{2,1,0:T(1,128)S(1)}, u32[]{:S(2)}, u32[]{:S(2)}) collective-permute-start(f32[3,1,1024]{2,1,0:T(1,128)S(1)} %get-tuple-element.268), channel_id=1, source_target_pairs={{8,0},{16,8},{24,16},{9,1},{17,9},{25,17},{10,2},{18,10},{26,18},{... | collective-permute-start | bytes 36872 | tf_op jit(solution)/shard_map/ppermute | solution.py:15
  14.7 26.3 %collective-permute-start.5 = (f32[3,1,1024]{2,1,0:T(1,128)S(1)}, f32[3,1,1024]{2,1,0:T(1,128)S(1)}, u32[]{:S(2)}, u32[]{:S(2)}) collective-permute-start(f32[3,1,1024]{2,1,0:T(1,128)S(1)} %get-tuple-element.267), channel_id=1, source_target_pairs={{0,8},{8,16},{16,24},{1,9},{9,17},{17,25},{2,10},{10,18},{18,26},{... | collective-permute-start | bytes 36872 | tf_op jit(solution)/shard_map/ppermute | solution.py:14
  36.2 12.6 %collective-permute-start.2 = (bf16[12,34,1]{2,1,0:T(8,128)(2,1)S(1)}, bf16[12,34,1]{2,1,0:T(8,128)(2,1)S(1)}, u32[]{:S(2)}, u32[]{:S(2)}) collective-permute-start(bf16[12,34,1]{2,1,0:T(8,128)(2,1)S(1)} %get-tuple-element.262), channel_id=1, source_target_pairs={{0,1},{1,2},{2,3},{3,4},{4,5},{5,6},{6,7},{8,9},{9,10},{10,11},{11... | collective-permute-start | bytes 2456 | tf_op jit(solution)/shard_map/ppermute | solution.py:14
  39.6 9.8 %collective-permute-start.3 = (bf16[12,34,1]{2,1,0:T(8,128)(2,1)S(1)}, bf16[12,34,1]{2,1,0:T(8,128)(2,1)}, u32[]{:S(2)}, u32[]{:S(2)}) collective-permute-start(bf16[12,34,1]{2,1,0:T(8,128)(2,1)S(1)} %get-tuple-element.261), channel_id=1, source_target_pairs={{1,0},{2,1},{3,2},{4,3},{5,4},{6,5},{7,6},{9,8},{10,9},{11,10},{12... | collective-permute-start | bytes 2456 | tf_op jit(solution)/shard_map/ppermute | solution.py:15
  41.7 12.4 %collective-permute-start.6 = (f32[3,34,1]{2,1,0:T(8,128)}, f32[3,34,1]{2,1,0:T(8,128)}, u32[]{:S(2)}, u32[]{:S(2)}) collective-permute-start(f32[3,34,1]{2,1,0:T(8,128)} %get-tuple-element.265), channel_id=1, source_target_pairs={{1,0},{2,1},{3,2},{4,3},{5,4},{6,5},{7,6},{9,8},{10,9},{11,10},{12... | collective-permute-start | bytes 1232 | tf_op jit(solution)/shard_map/ppermute | solution.py:15
  43.0 11.1 %collective-permute-start.7 = (f32[3,34,1]{2,1,0:T(8,128)}, f32[3,34,1]{2,1,0:T(8,128)}, u32[]{:S(2)}, u32[]{:S(2)}) collective-permute-start(f32[3,34,1]{2,1,0:T(8,128)} %get-tuple-element.266), channel_id=1, source_target_pairs={{0,1},{1,2},{2,3},{3,4},{4,5},{5,6},{6,7},{8,9},{9,10},{10,11},{11... | collective-permute-start | bytes 1232 | tf_op jit(solution)/shard_map/ppermute | solution.py:14
  48.8 0.7 copy-start.9
  53.8 1.5 copy-start.1
  53.8 1.5 copy-start.2
  53.8 1.5 copy-start.3
  53.8 1.5 copy-start.4
  53.8 1.5 copy-start.5
  53.8 1.5 copy-start.6
  53.8 1.5 copy-start.7
  53.8 1.5 copy-start.8
  56.9 12.1 %copy-start.10 = (f32[3,1024]{1,0:T(4,128)S(1)}, f32[3,1024]{1,0:T(4,128)}, u32[]{:S(2)}) copy-start(f32[3,1024]{1,0:T(4,128)} %get-tuple-element.242) | copy-start | bytes 36868
Sparse Core Ops, SparseCore 0:
  126.1 144.2 all-reduce.2
where the time goes:
time: 284 us; the launch traced here: 283 us
  waiting for transfers between devices  144 us (51%)
  local copies, waits for them, and re-layouts  55.7 us (20%)
  other arithmetic  47.1 us (17%)
  starting transfers between devices  22.5 us (8%)
  between operations  14 us (5%)
    psum x1, waiting for transfers between devices, body(): summed = lax.psum(point_buffer, ('wall', 'surf'))  144 us
    another operation x31, other arithmetic  31.4 us
    scatter-add x15, local copies, waits for them, and re-layouts, body(): window = window.at[:, offset:offset + columns].add(contrib)  28.6 us
    ppermute x4, starting transfers between devices, padded(): before = lax.ppermute(last, axis, up)  17.4 us
    reduce_sum x16, local copies, waits for them, and re-layouts, body(): contrib = jnp.sum(picked[None] * sensitivity, axis=1)  12.5 us
    gather x2, local copies, waits for them, and re-layouts, body(): return summed[:, my_slots]  5.78 us
  transfers between devices with their start and end apart: 9, of which 1 were waited for; matrix products, arithmetic and copies ran while one was open for 8% of the time, Pallas kernels for 0%

commit v1 on v0

v1 whole, which is shorter than its diff:
```python
import functools

import jax
import jax.numpy as jnp
from jax import lax
from jax.experimental import pallas as pl
from jax.experimental.pallas import tpu as pltpu
from jax.sharding import PartitionSpec as P

LANES = 128
NV = 15


def face(low, high):
    jumps = [low[6 + v] - high[6 + v] for v in range(6)]
    sums = [low[v] + high[v] for v in range(6)]
    along = sum(jumps[v] * sums[v] for v in range(6)) * 0.25
    across = sum(jumps[v] * (high[v] - low[v]) for v in range(6))
    half = 0.5 * sums[4]
    return [
        along * sums[1 + k] + half * jumps[1 + k] - across * (high[12 + k] - low[12 + k])
        for k in range(3)
    ]


def fold(tiles, sub):
    for bit in (1, 2, 4):
        clear = (sub & bit) == 0
        folded = []
        for a, b in zip(tiles[0::2], tiles[1::2]):
            folded.append(jnp.where(clear, a, b) + pltpu.roll(jnp.where(clear, b, a), bit, 0))
        tiles = folded
    return tiles[0]


def kernel(
    n_wall,
    n_surf,
    primal,
    adjoint,
    coords,
    foot_index,
    foot_weight,
    blanking,
    owner,
    out,
    q_in,
    a_in,
    x_in,
    index_in,
    weight_in,
    blank_in,
    owner_in,
    field,
    before,
    row_low,
    row_high,
    col_low,
    col_high,
    from_below,
    from_above,
    from_left,
    from_right,
    wall_h,
    surf_h,
    window,
    packet,
    arrived,
    partial,
    load_sem,
    halo_send,
    halo_recv,
    slot_send,
    slot_recv,
    wall_send,
    wall_recv,
):
    layers, columns = blank_in.shape
    chunks = columns // LANES
    groups = layers // 8
    w = lax.axis_index("wall")
    s = lax.axis_index("surf")

    loads = [
        pltpu.make_async_copy(src, dst, load_sem.at[i])
        for i, (src, dst) in enumerate(
            (
                (primal, q_in),
                (adjoint, a_in),
                (coords, x_in),
                (foot_index, index_in),
                (foot_weight, weight_in),
                (blanking, blank_in),
                (owner, owner_in),
            )
        )
    ]
    for load in loads:
        load.start()

    barrier = pltpu.get_barrier_semaphore()
    for step in range(1, n_wall):
        peer = lax.rem(w + step, n_wall)
        pl.semaphore_signal(barrier, inc=1, device_id=(peer, s), device_id_type=pl.DeviceIdType.MESH)
    for step in range(1, n_surf):
        peer = lax.rem(s + step, n_surf)
        pl.semaphore_signal(barrier, inc=1, device_id=(w, peer), device_id_type=pl.DeviceIdType.MESH)

    lane32 = lax.broadcasted_iota(jnp.int32, (layers, LANES), 1)
    lane = lax.broadcasted_iota(jnp.int32, (8, LANES), 1)
    sub = lax.broadcasted_iota(jnp.int32, (8, LANES), 0)

    t_low = jnp.zeros((layers, LANES), jnp.float32)
    t_high = jnp.zeros((layers, LANES), jnp.float32)
    for v in range(NV):
        if v in (0, 6, 12):
            loads[v // 6].wait()
        source = (q_in, a_in, x_in)[v // 6]
        previous = None
        for c in range(chunks):
            x = source[v % 6, :, c * LANES : (c + 1) * LANES].astype(jnp.float32)
            field[v, c, 8 : 8 + layers, :] = x
            row_low[v, c : c + 1, :] = x[0:1]
            row_high[v, c : c + 1, :] = x[layers - 1 : layers]
            rolled = pltpu.roll(x, 1, 1)
            before[v, c] = rolled if c == 0 else jnp.where(lane32 == 0, previous, rolled)
            previous = rolled
            if c == 0:
                t_low = jnp.where(lane32 == v, jnp.broadcast_to(x[:, 0:1], x.shape), t_low)
            if c == chunks - 1:
                t_high = jnp.where(
                    lane32 == v, jnp.broadcast_to(x[:, LANES - 1 : LANES], x.shape), t_high
                )
    col_low[...] = t_low
    col_high[...] = t_high

    pl.semaphore_wait(barrier, n_wall + n_surf - 2)

    def halo(number, src, dst, target):
        return pltpu.make_async_remote_copy(
            src_ref=src,
            dst_ref=dst,
            send_sem=halo_send.at[number],
            recv_sem=halo_recv.at[number],
            device_id=target,
            device_id_type=pl.DeviceIdType.MESH,
        )

    to_above = halo(0, row_high, from_below, (lax.rem(w + 1, n_wall), s))
    to_below = halo(1, row_low, from_above, (lax.rem(w + n_wall - 1, n_wall), s))
    to_right = halo(2, col_high, from_left, (w, lax.rem(s + 1, n_surf)))
    to_left = halo(3, col_low, from_right, (w, lax.rem(s + n_surf - 1, n_surf)))
    sends = (
        (to_above, w < n_wall - 1),
        (to_below, w > 0),
        (to_right, s < n_surf - 1),
        (to_left, s > 0),
    )
    receives = (
        (to_above, w > 0, from_below),
        (to_below, w < n_wall - 1, from_above),
        (to_right, s > 0, from_left),
        (to_left, s < n_surf - 1, from_right),
    )
    for copy, wanted in sends:
        pl.when(wanted)(copy.start)

    def interior(c, carry):
        for g in range(groups):
            rows = pl.ds(8 + 8 * g, 8)
            high = [field[v, c, rows, :] for v in range(NV)]
            low = [field[v, c, pl.ds(7 + 8 * g, 8), :] for v in range(NV)]
            for k, h in enumerate(face(low, high)):
                wall_h[k, c, pl.ds(8 * g, 8), :] = h
            low = [before[v, c, pl.ds(8 * g, 8), :] for v in range(NV)]
            for k, h in enumerate(face(low, high)):
                surf_h[k, c, pl.ds(8 * g, 8), :] = h
        return carry

    for v in range(NV):
        field[v, :, 0:8, :] = jnp.zeros((chunks, 8, LANES), jnp.float32)
    lax.fori_loop(0, chunks, interior, 0)
    window[...] = jnp.zeros_like(window)

    for copy, wanted, landing in receives:
        pl.when(wanted)(copy.wait_recv)

        @pl.when(jnp.logical_not(wanted))
        def _():
            landing[...] = jnp.zeros_like(landing)

    below = face([from_below[v] for v in range(NV)], [row_low[v] for v in range(NV)])
    above = face([row_high[v] for v in range(NV)], [from_above[v] for v in range(NV)])
    for k in range(3):
        for c in range(chunks):
            wall_h[k, c, 0:1, :] = below[k][c : c + 1]
            wall_h[k, c, layers : layers + 1, :] = above[k][c : c + 1]
    for g in range(groups):
        rows = pl.ds(8 * g, 8)
        left = from_left[rows, :]
        right = from_right[rows, :]
        left = [jnp.broadcast_to(left[:, v : v + 1], (8, LANES)) for v in range(NV)]
        right = [jnp.broadcast_to(right[:, v : v + 1], (8, LANES)) for v in range(NV)]
        inner = pl.ds(8 + 8 * g, 8)
        first = face(left, [field[v, 0, inner, :] for v in range(NV)])
        last = face([field[v, chunks - 1, inner, :] for v in range(NV)], right)
        for k in range(3):
            surf_h[k, 0, rows, :] = jnp.where(lane == 0, first[k], surf_h[k, 0, rows, :])
            surf_h[k, chunks, rows, :] = pltpu.roll(last[k], 1, 1)

    for load in loads[3:]:
        load.wait()

    def gather_points(c, carry):
        span = pl.ds(pl.multiple_of(c * LANES, LANES), LANES)
        sens, index, weight = [], [], []
        for g in range(groups):
            rows = pl.ds(8 * g, 8)
            live = blank_in[rows, span].astype(jnp.float32)
            index.append([index_in[t, rows, span] for t in range(2)])
            weight.append([live * weight_in[t, rows, span] for t in range(2)])
            sens.append(
                [
                    wall_h[k, c, rows, :]
                    - wall_h[k, c, pl.ds(8 * g + 1, 8), :]
                    + surf_h[k, c, rows, :]
                    - jnp.where(
                        lane == LANES - 1,
                        pltpu.roll(surf_h[k, c + 1, rows, :], LANES - 1, 1),
                        pltpu.roll(surf_h[k, c, rows, :], LANES - 1, 1),
                    )
                    for k in range(3)
                ]
            )
        sums = [[], [], []]
        for offset in range(16):
            total = [None] * 3
            for g in range(groups):
                picked = jnp.where(index[g][0] == offset, weight[g][0], 0.0) + jnp.where(
                    index[g][1] == offset, weight[g][1], 0.0
                )
                for k in range(3):
                    term = picked * sens[g][k]
                    total[k] = term if total[k] is None else total[k] + term
            for k in range(3):
                sums[k].append(total[k])
        for k in range(3):
            down = pltpu.roll(fold(sums[k][:8], sub), LANES - 8, 1, stride=1, stride_axis=0)
            up = pltpu.roll(fold(sums[k][8:], sub), 0, 1, stride=1, stride_axis=0)
            to_left = lane >= LANES - 8 + sub
            to_right = lane < sub
            window[k, c] += jnp.where(to_left, down, 0.0)
            window[k, c + 1] += jnp.where(to_left, 0.0, down) + jnp.where(to_right, 0.0, up)
            window[k, c + 2] += jnp.where(to_right, up, 0.0)
        return carry

    lax.fori_loop(0, chunks, gather_points, 0)

    points = [fold([window[k, c + 1] for c in range(chunks)], sub) for k in range(3)]
    over = [jnp.sum(window[k, 0] + window[k, chunks + 1], axis=0, keepdims=True) for k in range(3)]

    for r in range(n_surf // 8):
        local = owner_in[pl.ds(s + 8 * r * n_surf, 8, stride=n_surf), :] - s * columns
        place = local & (LANES - 1)
        chunk = local >> 7
        for k in range(3):
            value = jnp.zeros((8, LANES), jnp.float32)
            for c in range(chunks):
                row = jnp.broadcast_to(points[k][c : c + 1], (8, LANES))
                value = jnp.where(chunk == c, jnp.take_along_axis(row, place, axis=1), value)
            packet[pl.ds(64 * r + k, 8, stride=8), :] = value
            packet[pl.ds(64 * r + 3 + k, 8, stride=8), :] = jnp.broadcast_to(over[k], (8, LANES))

    def slot_copy(target, source):
        return pltpu.make_async_remote_copy(
            src_ref=packet.at[pl.ds(pl.multiple_of(target * 8, 8), 8), :],
            dst_ref=arrived.at[pl.ds(pl.multiple_of(source * 8, 8), 8), :],
            send_sem=slot_send.at[target],
            recv_sem=slot_recv.at[source],
            device_id=(w, target),
            device_id_type=pl.DeviceIdType.MESH,
        )

    peers = [lax.rem(s + step, n_surf) for step in range(1, n_surf)]
    for peer in peers:
        slot_copy(peer, s).start()
    mine = pl.ds(pl.multiple_of(s * 8, 8), 8)
    arrived[mine, :] = packet[mine, :]
    for peer in peers:
        slot_copy(peer, peer).wait_recv()

    parts = partial.at[w]
    over = [arrived[pl.ds(3 + k, n_surf, stride=8), :] for k in range(3)]
    for k in range(3):
        ahead = jnp.concatenate([over[k][n_surf - 1 :], over[k][: n_surf - 1]], axis=0)
        behind = jnp.concatenate([over[k][1:], over[k][:1]], axis=0)
        for r in range(n_surf // 8):
            block = sub + 8 * r
            local = owner_in[pl.ds(pl.multiple_of(s * n_surf, 8) + 8 * r, 8), :] - block * columns
            place = local & (LANES - 1)
            value = arrived[pl.ds(64 * r + k, 8, stride=8), :]
            first = jnp.take_along_axis(ahead[8 * r : 8 * r + 8], place, axis=1)
            last = jnp.take_along_axis(behind[8 * r : 8 * r + 8], place, axis=1)
            value = value + jnp.where(local < 8, first, 0.0)
            value = value + jnp.where(local >= columns - 8, last, 0.0)
            parts[k, 8 * r : 8 * r + 8, :] = value

    def wall_copy(target, source):
        return pltpu.make_async_remote_copy(
            src_ref=partial.at[w],
            dst_ref=partial.at[source],
            send_sem=wall_send.at[target],
            recv_sem=wall_recv.at[source],
            device_id=(target, s),
            device_id_type=pl.DeviceIdType.MESH,
        )

    walls = [lax.rem(w + step, n_wall) for step in range(1, n_wall)]
    for peer in walls:
        wall_copy(peer, w).start()
    for copy, wanted in sends:
        pl.when(wanted)(copy.wait_send)
    for peer in peers:
        slot_copy(peer, s).wait_send()
    for peer in walls:
        wall_copy(peer, peer).wait_recv()
    total = partial[0]
    for other in range(1, n_wall):
        total = total + partial[other]
    out[...] = total
    for peer in walls:
        wall_copy(peer, w).wait_send()


def body(primal, adjoint, coords, foot_index, foot_weight, blanking, owner_map):
    n_wall = lax.axis_size("wall")
    n_surf = lax.axis_size("surf")
    layers, columns = blanking.shape
    chunks = columns // LANES
    share = columns // n_surf
    owner = owner_map.reshape(n_surf * n_surf, share)
    if share < LANES:
        owner = jnp.pad(owner, ((0, 0), (0, LANES - share)))
    f32 = jnp.float32
    scratch = [
        pltpu.VMEM(primal.shape, primal.dtype),
        pltpu.VMEM(adjoint.shape, adjoint.dtype),
        pltpu.VMEM(coords.shape, coords.dtype),
        pltpu.VMEM(foot_index.shape, jnp.int32),
        pltpu.VMEM(foot_weight.shape, f32),
        pltpu.VMEM(blanking.shape, jnp.int32),
        pltpu.VMEM(owner.shape, jnp.int32),
        pltpu.VMEM((NV, chunks, layers + 8, LANES), f32),
        pltpu.VMEM((NV, chunks, layers, LANES), f32),
        pltpu.VMEM((NV, chunks, LANES), f32),
        pltpu.VMEM((NV, chunks, LANES), f32),
        pltpu.VMEM((layers, LANES), f32),
        pltpu.VMEM((layers, LANES), f32),
        pltpu.VMEM((NV, chunks, LANES), f32),
        pltpu.VMEM((NV, chunks, LANES), f32),
        pltpu.VMEM((layers, LANES), f32),
        pltpu.VMEM((layers, LANES), f32),
        pltpu.VMEM((3, chunks, layers + 8, LANES), f32),
        pltpu.VMEM((3, chunks + 1, layers, LANES), f32),
        pltpu.VMEM((3, chunks + 2, 8, LANES), f32),
        pltpu.VMEM((n_surf * 8, LANES), f32),
        pltpu.VMEM((n_surf * 8, LANES), f32),
        pltpu.VMEM((n_wall, 3, n_surf, LANES), f32),
        pltpu.SemaphoreType.DMA((7,)),
        pltpu.SemaphoreType.DMA((4,)),
        pltpu.SemaphoreType.DMA((4,)),
        pltpu.SemaphoreType.DMA((n_surf,)),
        pltpu.SemaphoreType.DMA((n_surf,)),
        pltpu.SemaphoreType.DMA((n_wall,)),
        pltpu.SemaphoreType.DMA((n_wall,)),
    ]
    summed = pl.pallas_call(
        functools.partial(kernel, n_wall, n_surf),
        out_shape=jax.ShapeDtypeStruct((3, n_surf, LANES), f32),
        in_specs=[pl.BlockSpec(memory_space=pl.ANY)] * 7,
        out_specs=pl.BlockSpec(memory_space=pltpu.VMEM),
        scratch_shapes=scratch,
        compiler_params=pltpu.CompilerParams(
            collective_id=0, has_side_effects=True, vmem_limit_bytes=32 * 1024 * 1024
        ),
    )(primal, adjoint, coords, foot_index, foot_weight, blanking, owner)
    return summed[:, :, :share].reshape(3, columns)


def solution(mesh):
    placed = (
        P(None, "wall", "surf"),
        P(None, "wall", "surf"),
        P(None, "wall", "surf"),
        P(None, "wall", "surf"),
        P(None, "wall", "surf"),
        P("wall", "surf"),
        P(),
    )
    return jax.shard_map(
        body, mesh=mesh, in_specs=placed, out_specs=P(None, "surf"), check_vma=False
    )
```

time: 284 us -> 25.9 us (0.09)
  waiting for transfers between devices: 144 us -> 0 us
  local copies, waits for them, and re-layouts: 55.7 us -> 7.16 us
  other arithmetic: 47.1 us -> 0 us
  starting transfers between devices: 22.5 us -> 0 us
  Pallas kernels: 0 us -> 18.4 us
  between operations: 14 us -> 0.02 us
    psum x1 -> x0, waiting for transfers between devices: 144 us -> none  [body(): summed = lax.psum(point_buffer, ('wall', 'surf'))]
    another operation x31 -> x0, other arithmetic: 31.4 us -> none
    scatter-add x15 -> x0, local copies, waits for them, and re-layouts: 28.6 us -> none  [body(): window = window.at[:, offset:offset + columns].add(contrib)]
    ppermute x8 -> x0, starting transfers between devices: 22.5 us -> none  [the longest x4 17.4 us: padded(): before = lax.ppermute(last, axis, up)]
    pallas_call x0 -> x1, Pallas kernels: none -> 18.4 us  [body(): pl.pallas_call(functools.partial(kernel, n_wall, n_surf), out_shape=jax.S...]
    reduce_sum x16 -> x0, local copies, waits for them, and re-layouts: 12.5 us -> none  [body(): contrib = jnp.sum(picked[None] * sensitivity, axis=1)]
    reduce_sum x4 -> x0, other arithmetic: 6.16 us -> none  [the longest x1 2.73 us: body(): picked = jnp.sum(jnp.where(foot_index == offset, weighted, 0.0), axis=0)]
    gather x2 -> x0, local copies, waits for them, and re-layouts: 5.78 us -> none  [body(): return summed[:, my_slots]]
  transfers between devices with their start and end apart: 9 -> 0, of which waited for: 1 -> 0; matrix products, arithmetic and copies ran while one was open for 8% -> 0% of each run, Pallas kernels for 0% -> 0%
where the time goes in v1:
time: 25.9 us; the launch traced here: 25.6 us
  Pallas kernels  18.4 us (71%)
  local copies, waits for them, and re-layouts  7.16 us (28%)
    pallas_call x1, Pallas kernels, body(): pl.pallas_call(functools.partial(kernel, n_wall, n_surf), out_shape=jax.S...  18.4 us
    unnamed x15, local copies, waits for them, and re-layouts  7.16 us

profile of v1, /device:TPU:0, one launch (start us, length us, event | category | flops | bytes accessed | tf_op | source)
XLA Modules:
  0.0 25.6 jit_solution(320822720077352896)
XLA Ops:
  0.0 0.0 copy-start
  0.0 1.0 %copy-done = bf16[6,32,1024]{2,1,0:T(8,128)(2,1)S(1)} copy-done((bf16[6,32,1024]{2,1,0:T(8,128)(2,1)S(1)}, bf16[6,32,1024]{2,1,0:T(8,128)(2,1)}, u32[]{:S(2)}) %copy-start) | copy-done | bytes 393240
  1.0 0.0 copy-start.1
  1.0 1.0 %copy-done.1 = bf16[6,32,1024]{2,1,0:T(8,128)(2,1)S(1)} copy-done((bf16[6,32,1024]{2,1,0:T(8,128)(2,1)S(1)}, bf16[6,32,1024]{2,1,0:T(8,128)(2,1)}, u32[]{:S(2)}) %copy-start.1) | copy-done | bytes 393240
  2.0 0.0 copy-start.2
  2.0 1.0 %copy-done.2 = f32[3,32,1024]{2,1,0:T(8,128)S(1)} copy-done((f32[3,32,1024]{2,1,0:T(8,128)S(1)}, f32[3,32,1024]{2,1,0:T(8,128)}, u32[]{:S(2)}) %copy-start.2) | copy-done | bytes 393240
  3.0 0.0 copy-start.3
  3.0 0.9 %copy-done.3 = s32[2,32,1024]{2,1,0:T(8,128)S(1)} copy-done((s32[2,32,1024]{2,1,0:T(8,128)S(1)}, s32[2,32,1024]{2,1,0:T(8,128)}, u32[]{:S(2)}) %copy-start.3) | copy-done | bytes 262168
  3.9 0.0 copy-start.4
  3.9 0.9 %copy-done.4 = f32[2,32,1024]{2,1,0:T(8,128)S(1)} copy-done((f32[2,32,1024]{2,1,0:T(8,128)S(1)}, f32[2,32,1024]{2,1,0:T(8,128)}, u32[]{:S(2)}) %copy-start.4) | copy-done | bytes 262168
  4.9 0.0 copy-start.5
  4.9 0.9 %copy-done.5 = s32[32,1024]{1,0:T(8,128)S(1)} copy-done((s32[32,1024]{1,0:T(8,128)S(1)}, s32[32,1024]{1,0:T(8,128)}, u32[]{:S(2)}) %copy-start.5) | copy-done | bytes 131096
  5.8 0.0 copy-start.6
  5.8 0.8 %copy-done.6 = s32[8192]{0:T(1024)S(1)} copy-done((s32[8192]{0:T(1024)S(1)}, s32[8192]{0:T(1024)}, u32[]{:S(2)}) %copy-start.6) | copy-done | bytes 32792
  6.6 18.4 %shard_map.73 = f32[3,8,128]{2,1,0:T(8,128)S(1)} custom-call(bf16[6,32,1024]{2,1,0:T(8,128)(2,1)S(1)} %copy-done, bf16[6,32,1024]{2,1,0:T(8,128)(2,1)S(1)} %copy-done.1, f32[3,32,1024]{2,1,0:T(8,128)S(1)} %copy-done.2, s32[2,32,1024]{2,1,0:T(8,128)S(1)} %copy-done.3, f32[2,32,1024]{2,1,0:T(8,128)S(1)} %copy-done.4, s32[32,1024]{1,0:T(8,128)S(1)} %copy-done.5, ...), custom_call_target="tpu_custom_call" | custom-call | tf_op jit(solution)/shard_map/pallas_call | solution.py:377
  25.0 0.6 %copy.10 = f32[1,3,8,128]{3,1,2,0:T(4,128)} copy(f32[1,3,8,128]{3,2,1,0:T(8,128)S(1)} %bitcast.5) | data formatting | bytes 24576
Async XLA Ops:
  0.0 1.0 %copy-start = (bf16[6,32,1024]{2,1,0:T(8,128)(2,1)S(1)}, bf16[6,32,1024]{2,1,0:T(8,128)(2,1)}, u32[]{:S(2)}) copy-start(bf16[6,32,1024]{2,1,0:T(8,128)(2,1)} %primal.1) | copy-start | bytes 1179652
  1.0 1.0 %copy-start.1 = (bf16[6,32,1024]{2,1,0:T(8,128)(2,1)S(1)}, bf16[6,32,1024]{2,1,0:T(8,128)(2,1)}, u32[]{:S(2)}) copy-start(bf16[6,32,1024]{2,1,0:T(8,128)(2,1)} %adjoint.1) | copy-start | bytes 1179652
  2.0 1.0 %copy-start.2 = (f32[3,32,1024]{2,1,0:T(8,128)S(1)}, f32[3,32,1024]{2,1,0:T(8,128)}, u32[]{:S(2)}) copy-start(f32[3,32,1024]{2,1,0:T(8,128)} %coords.1) | copy-start | bytes 1179652
  3.0 0.9 %copy-start.3 = (s32[2,32,1024]{2,1,0:T(8,128)S(1)}, s32[2,32,1024]{2,1,0:T(8,128)}, u32[]{:S(2)}) copy-start(s32[2,32,1024]{2,1,0:T(8,128)} %foot_index.1) | copy-start | bytes 786436
  3.9 0.9 %copy-start.4 = (f32[2,32,1024]{2,1,0:T(8,128)S(1)}, f32[2,32,1024]{2,1,0:T(8,128)}, u32[]{:S(2)}) copy-start(f32[2,32,1024]{2,1,0:T(8,128)} %foot_weight.1) | copy-start | bytes 786436
  4.9 0.9 %copy-start.5 = (s32[32,1024]{1,0:T(8,128)S(1)}, s32[32,1024]{1,0:T(8,128)}, u32[]{:S(2)}) copy-start(s32[32,1024]{1,0:T(8,128)} %blanking.1) | copy-start | bytes 393220
  5.8 0.8 %copy-start.6 = (s32[8192]{0:T(1024)S(1)}, s32[8192]{0:T(1024)}, u32[]{:S(2)}) copy-start(s32[8192]{0:T(1024)} %param.13) | copy-start | bytes 98308

commit v2 on v1

--- a/solution.py
+++ b/solution.py
@@ -66,14 +66,11 @@
     window,
     packet,
     arrived,
-    partial,
     load_sem,
     halo_send,
     halo_recv,
     slot_send,
     slot_recv,
-    wall_send,
-    wall_recv,
 ):
     layers, columns = blank_in.shape
     chunks = columns // LANES
@@ -99,12 +96,14 @@
         load.start()
 
     barrier = pltpu.get_barrier_semaphore()
-    for step in range(1, n_wall):
-        peer = lax.rem(w + step, n_wall)
-        pl.semaphore_signal(barrier, inc=1, device_id=(peer, s), device_id_type=pl.DeviceIdType.MESH)
-    for step in range(1, n_surf):
-        peer = lax.rem(s + step, n_surf)
-        pl.semaphore_signal(barrier, inc=1, device_id=(w, peer), device_id_type=pl.DeviceIdType.MESH)
+    peers = [
+        (lax.rem(w + up, n_wall), lax.rem(s + along, n_surf))
+        for along in range(n_surf)
+        for up in range(n_wall)
+        if up or along
+    ]
+    for peer in peers:
+        pl.semaphore_signal(barrier, inc=1, device_id=peer, device_id_type=pl.DeviceIdType.MESH)
 
     lane32 = lax.broadcasted_iota(jnp.int32, (layers, LANES), 1)
     lane = lax.broadcasted_iota(jnp.int32, (8, LANES), 1)
@@ -134,7 +133,7 @@
     col_low[...] = t_low
     col_high[...] = t_high
 
-    pl.semaphore_wait(barrier, n_wall + n_surf - 2)
+    pl.semaphore_wait(barrier, len(peers))
 
     def halo(number, src, dst, target):
         return pltpu.make_async_remote_copy(
@@ -271,26 +270,30 @@
             packet[pl.ds(64 * r + k, 8, stride=8), :] = value
             packet[pl.ds(64 * r + 3 + k, 8, stride=8), :] = jnp.broadcast_to(over[k], (8, LANES))
 
-    def slot_copy(target, source):
-        return pltpu.make_async_remote_copy(
-            src_ref=packet.at[pl.ds(pl.multiple_of(target * 8, 8), 8), :],
-            dst_ref=arrived.at[pl.ds(pl.multiple_of(source * 8, 8), 8), :],
-            send_sem=slot_send.at[target],
-            recv_sem=slot_recv.at[source],
-            device_id=(w, target),
+    me = pl.ds(pl.multiple_of((w * n_surf + s) * 8, 8), 8)
+    for peer in peers:
+        pltpu.make_async_remote_copy(
+            src_ref=packet.at[pl.ds(pl.multiple_of(peer[1] * 8, 8), 8), :],
+            dst_ref=arrived.at[me, :],
+            send_sem=slot_send,
+            recv_sem=slot_recv,
+            device_id=peer,
             device_id_type=pl.DeviceIdType.MESH,
-        )
-
-    peers = [lax.rem(s + step, n_surf) for step in range(1, n_surf)]
-    for peer in peers:
-        slot_copy(peer, s).start()
-    mine = pl.ds(pl.multiple_of(s * 8, 8), 8)
-    arrived[mine, :] = packet[mine, :]
-    for peer in peers:
-        slot_copy(peer, peer).wait_recv()
-
-    parts = partial.at[w]
-    over = [arrived[pl.ds(3 + k, n_surf, stride=8), :] for k in range(3)]
+        ).start()
+    arrived[me, :] = packet[pl.ds(pl.multiple_of(s * 8, 8), 8), :]
+    for copy, wanted in sends:
+        pl.when(wanted)(copy.wait_send)
+    others = arrived.at[pl.ds(0, 8 * len(peers)), :]
+    pltpu.make_async_copy(others, others, slot_recv).wait()
+
+    def from_all(row, first, count):
+        rows = [
+            arrived[pl.ds((other * n_surf + first) * 8 + row, count, stride=8), :]
+            for other in range(n_wall)
+        ]
+        return functools.reduce(lambda a, b: a + b, rows)
+
+    over = [from_all(3 + k, 0, n_surf) for k in range(3)]
     for k in range(3):
         ahead = jnp.concatenate([over[k][n_surf - 1 :], over[k][: n_surf - 1]], axis=0)
         behind = jnp.concatenate([over[k][1:], over[k][:1]], axis=0)
@@ -298,38 +301,13 @@
             block = sub + 8 * r
             local = owner_in[pl.ds(pl.multiple_of(s * n_surf, 8) + 8 * r, 8), :] - block * columns
             place = local & (LANES - 1)
-            value = arrived[pl.ds(64 * r + k, 8, stride=8), :]
+            value = from_all(k, 8 * r, 8)
             first = jnp.take_along_axis(ahead[8 * r : 8 * r + 8], place, axis=1)
             last = jnp.take_along_axis(behind[8 * r : 8 * r + 8], place, axis=1)
             value = value + jnp.where(local < 8, first, 0.0)
             value = value + jnp.where(local >= columns - 8, last, 0.0)
-            parts[k, 8 * r : 8 * r + 8, :] = value
-
-    def wall_copy(target, source):
-        return pltpu.make_async_remote_copy(
-            src_ref=partial.at[w],
-            dst_ref=partial.at[source],
-            send_sem=wall_send.at[target],
-            recv_sem=wall_recv.at[source],
-            device_id=(target, s),
-            device_id_type=pl.DeviceIdType.MESH,
-        )
-
-    walls = [lax.rem(w + step, n_wall) for step in range(1, n_wall)]
-    for peer in walls:
-        wall_copy(peer, w).start()
-    for copy, wanted in sends:
-        pl.when(wanted)(copy.wait_send)
-    for peer in peers:
-        slot_copy(peer, s).wait_send()
-    for peer in walls:
-        wall_copy(peer, peer).wait_recv()
-    total = partial[0]
-    for other in range(1, n_wall):
-        total = total + partial[other]
-    out[...] = total
-    for peer in walls:
-        wall_copy(peer, w).wait_send()
+            out[k, 8 * r : 8 * r + 8, :] = value
+    pltpu.make_async_copy(others, others, slot_send).wait()
 
 
 def body(primal, adjoint, coords, foot_index, foot_weight, blanking, owner_map):
@@ -364,15 +342,12 @@
         pltpu.VMEM((3, chunks + 1, layers, LANES), f32),
         pltpu.VMEM((3, chunks + 2, 8, LANES), f32),
         pltpu.VMEM((n_surf * 8, LANES), f32),
-        pltpu.VMEM((n_surf * 8, LANES), f32),
-        pltpu.VMEM((n_wall, 3, n_surf, LANES), f32),
+        pltpu.VMEM((n_wall * n_surf * 8, LANES), f32),
         pltpu.SemaphoreType.DMA((7,)),
         pltpu.SemaphoreType.DMA((4,)),
         pltpu.SemaphoreType.DMA((4,)),
-        pltpu.SemaphoreType.DMA((n_surf,)),
-        pltpu.SemaphoreType.DMA((n_surf,)),
-        pltpu.SemaphoreType.DMA((n_wall,)),
-        pltpu.SemaphoreType.DMA((n_wall,)),
+        pltpu.SemaphoreType.DMA,
+        pltpu.SemaphoreType.DMA,
     ]
     summed = pl.pallas_call(
         functools.partial(kernel, n_wall, n_surf),
@@ -381,7 +356,7 @@
         out_specs=pl.BlockSpec(memory_space=pltpu.VMEM),
         scratch_shapes=scratch,
         compiler_params=pltpu.CompilerParams(
-            collective_id=0, has_side_effects=True, vmem_limit_bytes=32 * 1024 * 1024
+            collective_id=0, has_side_effects=True, vmem_limit_bytes=60 * 1024 * 1024
         ),
     )(primal, adjoint, coords, foot_index, foot_weight, blanking, owner)
     return summed[:, :, :share].reshape(3, columns)

time: 25.9 us -> 18.1 us (0.70)
  local copies, waits for them, and re-layouts: 7.16 us -> 1.32 us
  Pallas kernels: 18.4 us -> 16.6 us
    unnamed x15 -> x1, local copies, waits for them, and re-layouts: 7.16 us -> 1.32 us
    pallas_call x1, Pallas kernels: 18.4 us -> 16.6 us  [body(): pl.pallas_call(functools.partial(kernel, n_wall, n_surf), out_shape=jax.S...]
where the time goes in v2:
time: 18.1 us; the launch traced here: 17.9 us
  Pallas kernels  16.6 us (92%)
  local copies, waits for them, and re-layouts  1.32 us (7%)
    pallas_call x1, Pallas kernels, body(): pl.pallas_call(functools.partial(kernel, n_wall, n_surf), out_shape=jax.S...  16.6 us
    unnamed x1, local copies, waits for them, and re-layouts  1.32 us

profile of v2, /device:TPU:0, one launch (start us, length us, event | category | flops | bytes accessed | tf_op | source)
XLA Modules:
  0.0 17.9 jit_solution(7217866653273565116)
XLA Ops:
  0.0 16.6 %shard_map.73 = f32[3,8,128]{2,1,0:T(8,128)} custom-call(bf16[6,32,1024]{2,1,0:T(8,128)(2,1)} %primal.1, bf16[6,32,1024]{2,1,0:T(8,128)(2,1)} %adjoint.1, f32[3,32,1024]{2,1,0:T(8,128)} %coords.1, s32[2,32,1024]{2,1,0:T(8,128)} %foot_index.1, f32[2,32,1024]{2,1,0:T(8,128)} %foot_weight.1, s32[32,1024]{1,0:T(8,128)} %blanking.1, s32[64,128]{1,0:T(8,128)} %bitcast.6), custom_call_target="tpu_custom_call" | custom-call | tf_op jit(solution)/shard_map/pallas_call | solution.py:352
  16.6 1.3 %copy.10 = f32[1,3,8,128]{3,1,2,0:T(4,128)} copy(f32[1,3,8,128]{3,2,1,0:T(8,128)} %bitcast.5) | data formatting | bytes 24576

commit v3 on v2

--- a/solution.py
+++ b/solution.py
@@ -178,7 +178,7 @@
 
     for v in range(NV):
         field[v, :, 0:8, :] = jnp.zeros((chunks, 8, LANES), jnp.float32)
-    lax.fori_loop(0, chunks, interior, 0)
+    lax.fori_loop(0, chunks, interior, 0, unroll=2)
     window[...] = jnp.zeros_like(window)
 
     for copy, wanted, landing in receives:
@@ -253,11 +253,12 @@
             window[k, c + 2] += jnp.where(to_right, up, 0.0)
         return carry
 
-    lax.fori_loop(0, chunks, gather_points, 0)
+    lax.fori_loop(0, chunks, gather_points, 0, unroll=True)
 
     points = [fold([window[k, c + 1] for c in range(chunks)], sub) for k in range(3)]
     over = [jnp.sum(window[k, 0] + window[k, chunks + 1], axis=0, keepdims=True) for k in range(3)]
 
+    spill = over[0] + pltpu.roll(over[1], 16, 1) + pltpu.roll(over[2], 32, 1)
     for r in range(n_surf // 8):
         local = owner_in[pl.ds(s + 8 * r * n_surf, 8, stride=n_surf), :] - s * columns
         place = local & (LANES - 1)
@@ -268,22 +269,22 @@
                 row = jnp.broadcast_to(points[k][c : c + 1], (8, LANES))
                 value = jnp.where(chunk == c, jnp.take_along_axis(row, place, axis=1), value)
             packet[pl.ds(64 * r + k, 8, stride=8), :] = value
-            packet[pl.ds(64 * r + 3 + k, 8, stride=8), :] = jnp.broadcast_to(over[k], (8, LANES))
-
-    me = pl.ds(pl.multiple_of((w * n_surf + s) * 8, 8), 8)
+        packet[pl.ds(64 * r + 3, 8, stride=8), :] = jnp.broadcast_to(spill, (8, LANES))
+
+    me = pl.ds(pl.multiple_of((w * n_surf + s) * 8, 8), 4)
     for peer in peers:
         pltpu.make_async_remote_copy(
-            src_ref=packet.at[pl.ds(pl.multiple_of(peer[1] * 8, 8), 8), :],
+            src_ref=packet.at[pl.ds(pl.multiple_of(peer[1] * 8, 8), 4), :],
             dst_ref=arrived.at[me, :],
             send_sem=slot_send,
             recv_sem=slot_recv,
             device_id=peer,
             device_id_type=pl.DeviceIdType.MESH,
         ).start()
-    arrived[me, :] = packet[pl.ds(pl.multiple_of(s * 8, 8), 8), :]
+    arrived[me, :] = packet[pl.ds(pl.multiple_of(s * 8, 8), 4), :]
     for copy, wanted in sends:
         pl.when(wanted)(copy.wait_send)
-    others = arrived.at[pl.ds(0, 8 * len(peers)), :]
+    others = arrived.at[pl.ds(0, 4 * len(peers)), :]
     pltpu.make_async_copy(others, others, slot_recv).wait()
 
     def from_all(row, first, count):
@@ -293,14 +294,14 @@
         ]
         return functools.reduce(lambda a, b: a + b, rows)
 
-    over = [from_all(3 + k, 0, n_surf) for k in range(3)]
+    spill = from_all(3, 0, n_surf)
+    ahead = jnp.concatenate([spill[n_surf - 1 :], spill[: n_surf - 1]], axis=0)
+    behind = jnp.concatenate([spill[1:], spill[:1]], axis=0)
     for k in range(3):
-        ahead = jnp.concatenate([over[k][n_surf - 1 :], over[k][: n_surf - 1]], axis=0)
-        behind = jnp.concatenate([over[k][1:], over[k][:1]], axis=0)
         for r in range(n_surf // 8):
             block = sub + 8 * r
             local = owner_in[pl.ds(pl.multiple_of(s * n_surf, 8) + 8 * r, 8), :] - block * columns
-            place = local & (LANES - 1)
+            place = (local + 16 * k) & (LANES - 1)
             value = from_all(k, 8 * r, 8)
             first = jnp.take_along_axis(ahead[8 * r : 8 * r + 8], place, axis=1)
             last = jnp.take_along_axis(behind[8 * r : 8 * r + 8], place, axis=1)

time: 18.1 us -> 16.8 us (0.928)
  Pallas kernels: 16.6 us -> 15.3 us
    pallas_call x1, Pallas kernels: 16.6 us -> 15.3 us  [body(): pl.pallas_call(functools.partial(kernel, n_wall, n_surf), out_shape=jax.S...]
where the time goes in v3:
time: 16.8 us; the launch traced here: 16.6 us
  Pallas kernels  15.3 us (91%)
  local copies, waits for them, and re-layouts  1.32 us (8%)
    pallas_call x1, Pallas kernels, body(): pl.pallas_call(functools.partial(kernel, n_wall, n_surf), out_shape=jax.S...  15.3 us
    unnamed x1, local copies, waits for them, and re-layouts  1.32 us

profile of v3, /device:TPU:0, one launch (start us, length us, event | category | flops | bytes accessed | tf_op | source)
XLA Modules:
  0.0 16.6 jit_solution(13467537357133320918)
XLA Ops:
  0.0 15.3 %shard_map.73 = f32[3,8,128]{2,1,0:T(8,128)} custom-call(bf16[6,32,1024]{2,1,0:T(8,128)(2,1)} %primal.1, bf16[6,32,1024]{2,1,0:T(8,128)(2,1)} %adjoint.1, f32[3,32,1024]{2,1,0:T(8,128)} %coords.1, s32[2,32,1024]{2,1,0:T(8,128)} %foot_index.1, f32[2,32,1024]{2,1,0:T(8,128)} %foot_weight.1, s32[32,1024]{1,0:T(8,128)} %blanking.1, s32[64,128]{1,0:T(8,128)} %bitcast.6), custom_call_target="tpu_custom_call" | custom-call | tf_op jit(solution)/shard_map/pallas_call | solution.py:353
  15.3 1.3 %copy.10 = f32[1,3,8,128]{3,1,2,0:T(4,128)} copy(f32[1,3,8,128]{3,2,1,0:T(8,128)} %bitcast.5) | data formatting | bytes 24576

commit v4 on v3

--- a/solution.py
+++ b/solution.py
@@ -180,40 +180,13 @@
         field[v, :, 0:8, :] = jnp.zeros((chunks, 8, LANES), jnp.float32)
     lax.fori_loop(0, chunks, interior, 0, unroll=2)
     window[...] = jnp.zeros_like(window)
-
-    for copy, wanted, landing in receives:
-        pl.when(wanted)(copy.wait_recv)
-
-        @pl.when(jnp.logical_not(wanted))
-        def _():
-            landing[...] = jnp.zeros_like(landing)
-
-    below = face([from_below[v] for v in range(NV)], [row_low[v] for v in range(NV)])
-    above = face([row_high[v] for v in range(NV)], [from_above[v] for v in range(NV)])
-    for k in range(3):
-        for c in range(chunks):
-            wall_h[k, c, 0:1, :] = below[k][c : c + 1]
-            wall_h[k, c, layers : layers + 1, :] = above[k][c : c + 1]
-    for g in range(groups):
-        rows = pl.ds(8 * g, 8)
-        left = from_left[rows, :]
-        right = from_right[rows, :]
-        left = [jnp.broadcast_to(left[:, v : v + 1], (8, LANES)) for v in range(NV)]
-        right = [jnp.broadcast_to(right[:, v : v + 1], (8, LANES)) for v in range(NV)]
-        inner = pl.ds(8 + 8 * g, 8)
-        first = face(left, [field[v, 0, inner, :] for v in range(NV)])
-        last = face([field[v, chunks - 1, inner, :] for v in range(NV)], right)
-        for k in range(3):
-            surf_h[k, 0, rows, :] = jnp.where(lane == 0, first[k], surf_h[k, 0, rows, :])
-            surf_h[k, chunks, rows, :] = pltpu.roll(last[k], 1, 1)
-
     for load in loads[3:]:
         load.wait()
 
-    def gather_points(c, carry):
-        span = pl.ds(pl.multiple_of(c * LANES, LANES), LANES)
+    def gather_points(c, chosen):
+        span = pl.ds(c * LANES, LANES)
         sens, index, weight = [], [], []
-        for g in range(groups):
+        for g in chosen:
             rows = pl.ds(8 * g, 8)
             live = blank_in[rows, span].astype(jnp.float32)
             index.append([index_in[t, rows, span] for t in range(2)])
@@ -234,7 +207,7 @@
         sums = [[], [], []]
         for offset in range(16):
             total = [None] * 3
-            for g in range(groups):
+            for g in range(len(chosen)):
                 picked = jnp.where(index[g][0] == offset, weight[g][0], 0.0) + jnp.where(
                     index[g][1] == offset, weight[g][1], 0.0
                 )
@@ -251,9 +224,40 @@
             window[k, c] += jnp.where(to_left, down, 0.0)
             window[k, c + 1] += jnp.where(to_left, 0.0, down) + jnp.where(to_right, 0.0, up)
             window[k, c + 2] += jnp.where(to_right, up, 0.0)
-        return carry
-
-    lax.fori_loop(0, chunks, gather_points, 0, unroll=True)
+
+    for c in range(1, chunks - 1):
+        gather_points(c, range(1, groups - 1))
+
+
+    for copy, wanted, landing in receives:
+        pl.when(wanted)(copy.wait_recv)
+
+        @pl.when(jnp.logical_not(wanted))
+        def _():
+            landing[...] = jnp.zeros_like(landing)
+
+    below = face([from_below[v] for v in range(NV)], [row_low[v] for v in range(NV)])
+    above = face([row_high[v] for v in range(NV)], [from_above[v] for v in range(NV)])
+    for k in range(3):
+        for c in range(chunks):
+            wall_h[k, c, 0:1, :] = below[k][c : c + 1]
+            wall_h[k, c, layers : layers + 1, :] = above[k][c : c + 1]
+    for g in range(groups):
+        rows = pl.ds(8 * g, 8)
+        left = from_left[rows, :]
+        right = from_right[rows, :]
+        left = [jnp.broadcast_to(left[:, v : v + 1], (8, LANES)) for v in range(NV)]
+        right = [jnp.broadcast_to(right[:, v : v + 1], (8, LANES)) for v in range(NV)]
+        inner = pl.ds(8 + 8 * g, 8)
+        first = face(left, [field[v, 0, inner, :] for v in range(NV)])
+        last = face([field[v, chunks - 1, inner, :] for v in range(NV)], right)
+        for k in range(3):
+            surf_h[k, 0, rows, :] = jnp.where(lane == 0, first[k], surf_h[k, 0, rows, :])
+            surf_h[k, chunks, rows, :] = pltpu.roll(last[k], 1, 1)
+
+    for c in range(chunks):
+        edge = c in (0, chunks - 1)
+        gather_points(c, range(groups) if edge else (0, groups - 1))
 
     points = [fold([window[k, c + 1] for c in range(chunks)], sub) for k in range(3)]
     over = [jnp.sum(window[k, 0] + window[k, chunks + 1], axis=0, keepdims=True) for k in range(3)]

time: 16.8 us -> 16.4 us (0.976)
  Pallas kernels: 15.3 us -> 14.8 us
    pallas_call x1, Pallas kernels: 15.3 us -> 14.8 us  [body(): pl.pallas_call(functools.partial(kernel, n_wall, n_surf), out_shape=jax.S...]
where the time goes in v4:
time: 16.4 us; the launch traced here: 16.1 us
  Pallas kernels  14.8 us (90%)
  local copies, waits for them, and re-layouts  1.32 us (8%)
    pallas_call x1, Pallas kernels, body(): pl.pallas_call(functools.partial(kernel, n_wall, n_surf), out_shape=jax.S...  14.8 us
    unnamed x1, local copies, waits for them, and re-layouts  1.32 us

profile of v4, /device:TPU:0, one launch (start us, length us, event | category | flops | bytes accessed | tf_op | source)
XLA Modules:
  0.0 16.1 jit_solution(15872726091521917509)
XLA Ops:
  0.0 14.8 %shard_map.73 = f32[3,8,128]{2,1,0:T(8,128)} custom-call(bf16[6,32,1024]{2,1,0:T(8,128)(2,1)} %primal.1, bf16[6,32,1024]{2,1,0:T(8,128)(2,1)} %adjoint.1, f32[3,32,1024]{2,1,0:T(8,128)} %coords.1, s32[2,32,1024]{2,1,0:T(8,128)} %foot_index.1, f32[2,32,1024]{2,1,0:T(8,128)} %foot_weight.1, s32[32,1024]{1,0:T(8,128)} %blanking.1, s32[64,128]{1,0:T(8,128)} %bitcast.6), custom_call_target="tpu_custom_call" | custom-call | tf_op jit(solution)/shard_map/pallas_call | solution.py:357
  14.8 1.3 %copy.10 = f32[1,3,8,128]{3,1,2,0:T(4,128)} copy(f32[1,3,8,128]{3,2,1,0:T(8,128)} %bitcast.5) | data formatting | bytes 24576

commit v5 on v4

--- a/solution.py
+++ b/solution.py
@@ -92,7 +92,7 @@
             )
         )
     ]
-    for load in loads:
+    for load in loads[:3]:
         load.start()
 
     barrier = pltpu.get_barrier_semaphore()
@@ -105,6 +105,9 @@
     for peer in peers:
         pl.semaphore_signal(barrier, inc=1, device_id=peer, device_id_type=pl.DeviceIdType.MESH)
 
+    for load in loads[3:]:
+        load.start()
+
     lane32 = lax.broadcasted_iota(jnp.int32, (layers, LANES), 1)
     lane = lax.broadcasted_iota(jnp.int32, (8, LANES), 1)
     sub = lax.broadcasted_iota(jnp.int32, (8, LANES), 0)
@@ -115,21 +118,16 @@
         if v in (0, 6, 12):
             loads[v // 6].wait()
         source = (q_in, a_in, x_in)[v // 6]
-        previous = None
+        bottom = source[v % 6, 0:16, :].astype(jnp.float32)
+        top = source[v % 6, layers - 16 : layers, :].astype(jnp.float32)
         for c in range(chunks):
-            x = source[v % 6, :, c * LANES : (c + 1) * LANES].astype(jnp.float32)
-            field[v, c, 8 : 8 + layers, :] = x
-            row_low[v, c : c + 1, :] = x[0:1]
-            row_high[v, c : c + 1, :] = x[layers - 1 : layers]
-            rolled = pltpu.roll(x, 1, 1)
-            before[v, c] = rolled if c == 0 else jnp.where(lane32 == 0, previous, rolled)
-            previous = rolled
-            if c == 0:
-                t_low = jnp.where(lane32 == v, jnp.broadcast_to(x[:, 0:1], x.shape), t_low)
-            if c == chunks - 1:
-                t_high = jnp.where(
-                    lane32 == v, jnp.broadcast_to(x[:, LANES - 1 : LANES], x.shape), t_high
-                )
+            span = slice(c * LANES, (c + 1) * LANES)
+            row_low[v, c : c + 1, :] = bottom[0:1, span]
+            row_high[v, c : c + 1, :] = top[15:16, span]
+        x = source[v % 6, :, 0:LANES].astype(jnp.float32)
+        t_low = jnp.where(lane32 == v, jnp.broadcast_to(x[:, 0:1], x.shape), t_low)
+        x = source[v % 6, :, columns - LANES : columns].astype(jnp.float32)
+        t_high = jnp.where(lane32 == v, jnp.broadcast_to(x[:, LANES - 1 : LANES], x.shape), t_high)
     col_low[...] = t_low
     col_high[...] = t_high
 
@@ -177,6 +175,14 @@
         return carry
 
     for v in range(NV):
+        source = (q_in, a_in, x_in)[v // 6]
+        previous = None
+        for c in range(chunks):
+            x = source[v % 6, :, c * LANES : (c + 1) * LANES].astype(jnp.float32)
+            field[v, c, 8 : 8 + layers, :] = x
+            rolled = pltpu.roll(x, 1, 1)
+            before[v, c] = rolled if c == 0 else jnp.where(lane32 == 0, previous, rolled)
+            previous = rolled
         field[v, :, 0:8, :] = jnp.zeros((chunks, 8, LANES), jnp.float32)
     lax.fori_loop(0, chunks, interior, 0, unroll=2)
     window[...] = jnp.zeros_like(window)

time: 16.4 us -> 16.3 us (level)
  no operation moved by 1% of the time
where the time goes in v5:
time: 16.3 us; the launch traced here: 16.1 us
  Pallas kernels  14.8 us (91%)
  local copies, waits for them, and re-layouts  1.32 us (8%)
    pallas_call x1, Pallas kernels, body(): pl.pallas_call(functools.partial(kernel, n_wall, n_surf), out_shape=jax.S...  14.8 us
    unnamed x1, local copies, waits for them, and re-layouts  1.32 us

profile of v5, /device:TPU:0, one launch (start us, length us, event | category | flops | bytes accessed | tf_op | source)
XLA Modules:
  0.0 16.1 jit_solution(14386525923562208100)
XLA Ops:
  0.0 14.8 %shard_map.73 = f32[3,8,128]{2,1,0:T(8,128)} custom-call(bf16[6,32,1024]{2,1,0:T(8,128)(2,1)} %primal.1, bf16[6,32,1024]{2,1,0:T(8,128)(2,1)} %adjoint.1, f32[3,32,1024]{2,1,0:T(8,128)} %coords.1, s32[2,32,1024]{2,1,0:T(8,128)} %foot_index.1, f32[2,32,1024]{2,1,0:T(8,128)} %foot_weight.1, s32[32,1024]{1,0:T(8,128)} %blanking.1, s32[64,128]{1,0:T(8,128)} %bitcast.6), custom_call_target="tpu_custom_call" | custom-call | tf_op jit(solution)/shard_map/pallas_call | solution.py:363
  14.8 1.3 %copy.10 = f32[1,3,8,128]{3,1,2,0:T(4,128)} copy(f32[1,3,8,128]{3,2,1,0:T(8,128)} %bitcast.5) | data formatting | bytes 24576
